TPU v7x, 128 devices: a whole 4x4x4 slice. The times are simulated.
128 devices in a mesh: dp: 16 (over z, x), tensor: 8 (over y, core).
Axes of the slice: x: 4, y: 4, z: 4, core: 2. Of those that a mesh axis runs over, the one named last changes fastest.
Arguments:
- activations: bfloat16 [16384, 8192], P('dp'), may hold values from -6 to 6
- output_grads: bfloat16 [16384, 28672], P('dp', 'tensor'), may hold values from -0.046875 to 0.046875
- basis: bfloat16 [8192, 512], P('dp', 'tensor'), may hold values from -0.0625 to 0.0625
- first_in: float32 [512, 28672], P('dp', 'tensor'), may hold values from -6 to 6
- second_in: float32 [512, 28672], P('dp', 'tensor'), may hold values from 0.2 to 2
Outputs:
- projected_grad: float32 [512, 28672], P('dp', 'tensor')
- first_out: float32 [512, 28672], P('dp', 'tensor')
- second_out: float32 [512, 28672], P('dp', 'tensor')
- update: bfloat16 [8192, 28672], P('dp', 'tensor')
All inputs are finite; a program needn't handle non-finite values.
Results may differ from a plain program's by a relative error of at most 0.0049.
Values may be sent and summed in bfloat16 or wider, within the bound.
A program may use at most 128 MiB of HBM per device.

v0:
```python
import jax
import jax.numpy as jnp
from jax import lax
from jax.sharding import PartitionSpec as P

STEP = 1000


beta_one = 0.9
beta_two = 0.999
adam_eps = 1e-08


def local(activations, output_grads, basis, first_in, second_in):
    rows_block = lax.all_gather(basis, "tensor", axis=1, tiled=True)
    columns = activations
    projected = jnp.dot(
        columns,
        lax.all_gather(rows_block, "dp", axis=0, tiled=True),
        preferred_element_type=jnp.float32,
    ).astype(jnp.bfloat16)
    projected_grad = lax.psum_scatter(
        jnp.einsum("tr,tf->rf", projected, output_grads, preferred_element_type=jnp.float32),
        "dp",
        scatter_dimension=0,
        tiled=True,
    )
    first_out = beta_one * first_in + (1.0 - beta_one) * projected_grad
    second_out = beta_two * second_in + (1.0 - beta_two) * projected_grad * projected_grad
    first_hat = first_out / (1.0 - beta_one**STEP)
    second_hat = second_out / (1.0 - beta_two**STEP)
    normalized = (first_hat / (jnp.sqrt(second_hat) + adam_eps)).astype(jnp.bfloat16)
    empty_update = jnp.zeros((rows_block.shape[0], normalized.shape[1]), jnp.float32)
    piece = lax.all_gather(normalized, "dp", axis=0, tiled=True)
    columns = lax.slice_in_dim(rows_block, 0, piece.shape[0], axis=1)
    update = (empty_update + jnp.dot(columns, piece, preferred_element_type=jnp.float32)).astype(
        jnp.bfloat16
    )
    return (projected_grad, first_out, second_out, update)


def solution(mesh):
    in_specs = (
        P("dp", None),
        P("dp", "tensor"),
        P("dp", "tensor"),
        P("dp", "tensor"),
        P("dp", "tensor"),
    )
    out_specs = (P("dp", "tensor"), P("dp", "tensor"), P("dp", "tensor"), P("dp", "tensor"))
    return jax.shard_map(local, mesh=mesh, in_specs=in_specs, out_specs=out_specs, check_vma=False)
```

profile of v0, /device:TPU:0, one launch (start us, length us, event | category | flops | bytes accessed | tf_op | source)
XLA Modules:
  0.0 286.7 jit_solution(11127291770696902155)
XLA Ops:
  7.2 0.0 all-gather.3.cloned.1.call-start
  7.2 15.0 %all_gather.9 = bf16[512,512]{0,1:T(8,128)(2,1)} all-gather(bf16[512,64]{0,1:T(8,128)(2,1)} %param.7), channel_id=1, replica_groups=mesh['dp'=16,'tensor'=8] {'tensor'}, dimensions={1}, use_global_device_ids=true | all-gather | bytes 589824 | tf_op jit(solution)/shard_map/all_gather | solution.py:15
  22.2 0.0 all-gather.3.cloned.1.call-update
  22.2 0.0 reduce-scatter.2.cloned.1.call-start
  22.3 80.3 %all-gather.3.cloned.1.call-done = bf16[8192,512]{0,1:T(8,128)(2,1)} async-done(((bf16[512,512]{0,1:T(8,128)(2,1)}), bf16[8192,512]{0,1:T(8,128)(2,1)}) %all-gather.3.cloned.1.call-update) | async-done | bytes 8388624 | tf_op jit(solution)/shard_map/all_gather | solution.py:19
  102.6 31.3 %fusion.2 = f32[512,3584]{1,0:T(8,128)} fusion(bf16[1024,3584]{1,0:T(8,128)(2,1)} %param.6, bf16[1024,8192]{1,0:T(8,128)(2,1)} %param.5, bf16[8192,512]{0,1:T(8,128)(2,1)} %all-gather.3.cloned.1.call-done), kind=kOutput, calls=%fused_computation.7 | convolution fusion | flops 12348555264 | bytes 39845888 | tf_op jit(solution)/shard_map/tr,tf->rf/dot_general | solution.py:23
  133.9 0.0 copy-start.1
  133.9 0.0 copy-start.2
  133.9 0.0 copy-start
  133.9 0.0 reduce-scatter.2.cloned.1.call-update
  133.9 0.0 all-gather.5.cloned.1.call-start
  134.0 82.3 %reduce-scatter.2.cloned.1.call-done = f32[32,3584]{1,0:T(8,128)} async-done(((f32[512,3584]{1,0:T(8,128)}), f32[32,3584]{1,0:T(8,128)}) %reduce-scatter.2.cloned.1.call-update) | async-done | bytes 458768 | tf_op jit(solution)/shard_map/reduce_scatter | solution.py:22
  216.2 0.0 copy-done.1
  216.3 0.0 copy-done.2
  216.3 2.1 divide_convert_fusion
  218.4 0.0 all-gather.5.cloned.1.call-update
  218.4 49.9 %all-gather.5.cloned.1.call-done = bf16[512,3584]{1,0:T(8,128)(2,1)} async-done(((bf16[32,3584]{1,0:T(8,128)(2,1)}), bf16[512,3584]{1,0:T(8,128)(2,1)}) %all-gather.5.cloned.1.call-update) | async-done | bytes 3670032 | tf_op jit(solution)/shard_map/all_gather | solution.py:34
  268.3 0.0 copy-done
  268.3 6.0 %fusion = bf16[512,3584]{0,1:T(8,128)(2,1)} fusion(bf16[512,3584]{1,0:T(8,128)(2,1)} %all-gather.5.cloned.1.call-done, bf16[512,512]{0,1:T(8,128)(2,1)S(1)} %copy-done), kind=kOutput, calls=%fused_computation.1 | convolution fusion | flops 1880883200 | bytes 7864320 | tf_op jit(solution)/shard_map/dot_general | solution.py:36
  274.3 5.9 %copy.9 = bf16[512,3584]{1,0:T(8,128)(2,1)} copy(bf16[512,3584]{0,1:T(8,128)(2,1)} %fusion) | data formatting | bytes 7340032
Async XLA Ops:
  7.2 95.4 %all-gather.3.cloned.1.call-start = ((), (), s32[]{:S(2)}) async-start(), calls=%async_computation.1 | async-start | bytes 8912896 | tf_op jit(solution)/shard_map/all_gather | solution.py:19
  22.2 194.0 %reduce-scatter.2.cloned.1.call-start = ((), (), s32[]{:S(2)}) async-start(), calls=%async_computation.2 | async-start | bytes 7798784 | tf_op jit(solution)/shard_map/reduce_scatter | solution.py:22
  133.9 82.4 %copy-start.1 = (f32[32,3584]{1,0:T(8,128)S(1)}, f32[32,3584]{1,0:T(8,128)}, u32[]{:S(2)}) copy-start(f32[32,3584]{1,0:T(8,128)} %param.9) | copy-start | bytes 1376260
  133.9 82.4 %copy-start.2 = (f32[32,3584]{1,0:T(8,128)S(1)}, f32[32,3584]{1,0:T(8,128)}, u32[]{:S(2)}) copy-start(f32[32,3584]{1,0:T(8,128)} %param.8) | copy-start | bytes 1376260
  133.9 134.4 %copy-start = (bf16[512,512]{0,1:T(8,128)(2,1)S(1)}, bf16[512,512]{0,1:T(8,128)(2,1)}, u32[]{:S(2)}) copy-start(bf16[512,512]{0,1:T(8,128)(2,1)} %all_gather.9) | copy-start | bytes 1572868
  133.9 134.4 %all-gather.5.cloned.1.call-start = ((), (), s32[]{:S(2)}) async-start(), calls=%async_computation.3 | async-start | bytes 3899392 | tf_op jit(solution)/shard_map/all_gather | solution.py:34
Sparse Core Ops, SparseCore 0:
  22.4 80.1 all-gather.2
  134.0 82.1 reduce-scatter.1
  219.2 49.0 all-gather.4
where the time goes:
time: 287 us
  waiting for transfers between devices  212 us (74%)
  matrix products  37.3 us (13%)
  blocking collectives  15 us (5%)
  between operations  13.8 us (5%)
  local copies, waits for them, and re-layouts  5.92 us (2%)
    reduce_scatter x1, waiting for transfers between devices, local(): lax.psum_scatter(jnp.einsum('tr,tf->rf', projected, output_grads, preferr...  82.3 us
    all_gather x1, waiting for transfers between devices, local(): lax.all_gather(rows_block, 'dp', axis=0, tiled=True)  80.3 us
    all_gather x1, waiting for transfers between devices, local(): piece = lax.all_gather(normalized, 'dp', axis=0, tiled=True)  49.9 us
    dot_general x1, matrix products, local(): jnp.einsum('tr,tf->rf', projected, output_grads, preferred_element_type=j...  31.3 us
    all_gather x1, blocking collectives, local(): rows_block = lax.all_gather(basis, 'tensor', axis=1, tiled=True)  15 us
    dot_general x1, matrix products, local(): jnp.dot(columns, piece, preferred_element_type=jnp.float32)  5.95 us
    unnamed x7, local copies, waits for them, and re-layouts  5.92 us
  transfers between devices with their start and end apart: 3, of which 3 were waited for; matrix products, arithmetic and copies ran while one was open for 0% of the time, Pallas kernels for 0%

commit v1 on v0

v1 whole, which is shorter than its diff:
```python
import functools

import jax
import jax.numpy as jnp
from jax import lax
from jax.experimental import pallas as pl
from jax.experimental.pallas import tpu as pltpu
from jax.sharding import PartitionSpec as P

STEP = 1000

beta_one = 0.9
beta_two = 0.999
adam_eps = 1e-08

MESH = pl.DeviceIdType.MESH
BF = jnp.bfloat16
F32 = jnp.float32

CHUNKS = 7
SIDE = 4
TO = (1, -1, 2)
FROM = (0, -1, 1, 2)

ORDER = [
    (0, 0), (0, 1), (0, 2), (0, 3), (0, 4), (0, 5), (1, 0), (1, 1), (0, 6), (1, 2),
    (1, 3), (1, 4), (1, 5), (2, 0), (2, 1), (1, 6), (2, 2), (2, 3), (2, 4), (2, 5),
    (3, 0), (3, 1), (2, 6), (3, 2), (3, 3), (3, 4), (3, 5), (4, 0), (4, 1), (3, 6),
    (4, 2), (4, 3), (4, 4), (4, 5), (5, 0), (5, 1), (4, 6), (5, 2), (5, 3), (5, 4),
    (5, 5), (6, 0), (6, 1), (5, 6), (6, 2), (6, 3), (6, 4), (6, 5), (6, 6),
]


def adam(grad, first, second):
    first_out = beta_one * first + (1.0 - beta_one) * grad
    second_out = beta_two * second + (1.0 - beta_two) * grad * grad
    return first_out, second_out


def step_of(first_out, second_out):
    first_hat = first_out / (1.0 - beta_one**STEP)
    second_hat = second_out / (1.0 - beta_two**STEP)
    return (first_hat / (jnp.sqrt(second_hat) + adam_eps)).astype(BF)


def exchange(
    acts, grads, basis, first, second,
    norm_out, rows_out, grad_out,
    act_v, grads_v, basis_v, first_v, second_v, packs, rows_packs, rows_v, acc, turned,
    part, send1, send2, send3, recv1, recv2, recv3, norm, grad_v,
    load_s, w1s, w1r, w2s, w2r, bs, br, ys, yr, s1, r1, s2, r2, s3, r3, s5, r5, s7, r7, s8, r8,
    out_s,
):
    dp, tensor = lax.axis_index("dp"), lax.axis_index("tensor")
    z, x, y, core = dp // SIDE, dp % SIDE, tensor // 2, tensor % 2
    width = grads_v.shape[2]
    half = width // 2

    def near(at, step):
        return lax.rem(at + step + SIDE, SIDE)

    def along(axis, step):
        if axis == "z":
            return (near(z, step) * SIDE + x, tensor)
        if axis == "x":
            return (z * SIDE + near(x, step), tensor)
        if axis == "y":
            return (dp, near(y, step) * 2 + core)
        return (dp, y * 2 + (1 - core))

    sent = []

    def send(src, dst, ssem, rsem, device):
        copy = pltpu.make_async_remote_copy(
            src_ref=src, dst_ref=dst, send_sem=ssem, recv_sem=rsem,
            device_id=device, device_id_type=MESH,
        )
        copy.start()
        sent.append(copy)
        return copy

    def got(ref, ssem, rsem, device):
        pltpu.make_async_remote_copy(
            src_ref=ref, dst_ref=ref, send_sem=ssem, recv_sem=rsem,
            device_id=device, device_id_type=MESH,
        ).wait_recv()

    def load(src, dst, n):
        copy = pltpu.make_async_copy(src, dst, load_s.at[n])
        copy.start()
        return copy

    order = [(0, 0), (0, 1), (0, 2), (1, 0), (2, 0), (0, 3), (3, 0)]
    order += [(a, b) for a in (1, 2) for b in (1, 2)]
    order += [(1, 3), (2, 3), (3, 1), (3, 2), (3, 3)]
    depth = act_v.shape[2]
    loaded_basis = load(basis, basis_v, 0)
    loaded_acts = []
    for n, (a, b) in enumerate(order):
        block = near(z, FROM[a]) * SIDE + near(x, FROM[b])
        columns = pl.ds(pl.multiple_of(block * depth, depth), depth)
        loaded_acts.append(load(acts.at[:, columns], act_v.at[n], 1 + n))
    loaded_grads = [
        load(grads.at[:, pl.ds(k * width, width)], grads_v.at[k], 17 + k) for k in range(CHUNKS)
    ]
    loaded_first = load(first, first_v, 17 + CHUNKS)
    loaded_second = load(second, second_v, 18 + CHUNKS)

    barrier = pltpu.get_barrier_semaphore()
    partners = [along(axis, step) for axis in "zxy" for step in TO] + [along("core", 1)]
    for device in partners:
        pl.semaphore_signal(barrier, inc=1, device_id=device, device_id_type=MESH)
    loaded_basis.wait()
    top = depth // 2
    pack = jnp.concatenate([basis_v[:top], basis_v[top:]], axis=1)
    packs[z, x] = pack
    rows_packs[tensor] = pack
    pl.semaphore_wait(barrier, len(partners))

    ends = (pl.ds(0, top // 2), pl.ds(top // 2, top // 2))

    def spot(path, m, i):
        a, b = (i, m) if path == 0 else (m, i)
        return packs.at[near(z, FROM[a]), near(x, FROM[b]), ends[path]]

    lead, trail = ("x", "z"), ("z", "x")
    for path in (0, 1):
        for i in range(3):
            send(spot(path, 0, 0), spot(path, 0, 0), w1s.at[path, i], w1r.at[path, i], along(lead[path], TO[i]))

    def onward(path, m):
        for i in range(3):
            send(spot(path, m, 0), spot(path, m, 0), w2s.at[path, m, i], w2r.at[path, m, i], along(trail[path], TO[i]))

    onward(0, 0)
    onward(1, 0)

    def spread(buffer, ssem, rsem):
        own = buffer.at[tensor]
        send(own, own, ssem.at[0], rsem.at[0], along("core", 1))
        for i in range(3):
            send(own, own, ssem.at[1 + i], rsem.at[1 + i], along("y", TO[i]))

    def forward(buffer, ssem, rsem):
        for i in range(3):
            block = buffer.at[near(y, FROM[1 + i]) * 2 + core]
            got(block, ssem.at[1 + i], rsem.at[1 + i], along("y", TO[i]))
            send(block, block, ssem.at[4 + i], rsem.at[4 + i], along("core", 1))

    def collected(buffer, ssem, rsem):
        for n in (0, 4, 5, 6):
            got(buffer.at[0], ssem.at[n], rsem.at[n], along("core", 1))

    spread(rows_packs, bs, br)

    def project(n):
        a, b = order[n]
        loaded_acts[n].wait()
        weights = packs[near(z, FROM[a]), near(x, FROM[b])]
        for side in (0, 1):
            term = jnp.dot(
                act_v[n, :, side * top : (side + 1) * top], weights, preferred_element_type=F32
            )
            acc[side] = term if n == 0 else acc[side] + term

    def arrived(n):
        a, b = order[n]
        for path, m, i in ((0, b, a), (1, a, b)):
            if i > 0:
                got(spot(path, m, i), w2s.at[path, m, i - 1], w2r.at[path, m, i - 1], along(trail[path], 1))

    def first_hop(i):
        for path in (0, 1):
            got(spot(path, i, 0), w1s.at[path, i - 1], w1r.at[path, i - 1], along(lead[path], 1))
            onward(path, i)

    project(0)
    for i in (1, 2, 3):
        first_hop(i)
    for n in range(1, len(order)):
        arrived(n)
        project(n)

    rank = turned.shape[1]
    total = acc[0] + pltpu.roll(acc[1], rank, 1)
    turned[tensor] = total.T[:rank].astype(BF)
    spread(turned, ys, yr)
    forward(rows_packs, bs, br)
    forward(turned, ys, yr)
    collected(rows_packs, bs, br)
    for n in range(SIDE):
        even, odd = rows_packs[2 * n], rows_packs[2 * n + 1]
        lanes = pl.ds(n * 2 * rank, 2 * rank)
        rows_v[:top, lanes] = jnp.concatenate([even[:, :rank], odd[:, :rank]], axis=1)
        rows_v[top:, lanes] = jnp.concatenate([even[:, rank:], odd[:, rank:]], axis=1)
    stores = []

    def store(src, dst, n):
        copy = pltpu.make_async_copy(src, dst, out_s.at[n])
        copy.start()
        stores.append(copy)

    store(rows_v, rows_out, CHUNKS)
    loaded_first.wait()
    loaded_second.wait()
    collected(turned, ys, yr)

    axes = (("z", "x"), ("x", "z"))
    places = ((z, x), (x, z))

    def lanes_of(path):
        return pl.ds(path * half, half)

    def slab(ref, path, place, low=0, count=SIDE):
        if path == 0:
            return ref.at[place, pl.ds(low, count)]
        return ref.at[pl.ds(low, count), place]

    def partial(path, k, place, low=0, count=SIDE):
        if path == 0:
            return part[k, place, low : low + count, :, lanes_of(path)]
        return part[k, low : low + count, place, :, lanes_of(path)]

    def columns_of(path, k):
        return pl.ds(k * width + path * half, half)

    def stage0(k):
        loaded_grads[k].wait()
        lhs = turned[...].reshape(2 * SIDE * rank, turned.shape[2])
        product = jnp.dot(lhs, grads_v[k], preferred_element_type=F32)
        part[k] = product.reshape(part.shape[1:])
        for path in (0, 1):
            far = near(places[path][0], 2)
            for d in (0, 1):
                send1[path, k, d] = partial(path, k, far, 2 * d, 2).astype(BF)
                send(send1.at[path, k, d], recv1.at[path, k, d], s1.at[path, k, d], r1.at[path, k, d], along(axes[path][0], TO[d]))

    def stage1(k):
        for path in (0, 1):
            for d in (0, 1):
                got(recv1.at[path, k, d], s1.at[path, k, d], r1.at[path, k, d], along(axes[path][0], TO[d]))
                to = near(places[path][0], TO[d])
                joined = partial(path, k, to, 2 * d, 2) + recv1[path, k, d].astype(F32)
                send2[path, k, d, 2 * d : 2 * d + 2] = joined.astype(BF)
                other = 2 - 2 * d
                send2[path, k, d, other : other + 2] = partial(path, k, to, other, 2).astype(BF)
                send(send2.at[path, k, d], recv2.at[path, k, d], s2.at[path, k, d], r2.at[path, k, d], along(axes[path][0], TO[d]))

    def stage2(k):
        for path in (0, 1):
            here, there = places[path]
            for d in (0, 1):
                got(recv2.at[path, k, d], s2.at[path, k, d], r2.at[path, k, d], along(axes[path][0], TO[d]))
            total = partial(path, k, here) + recv2[path, k, 0].astype(F32) + recv2[path, k, 1].astype(F32)
            if path == 0:
                part[k, here, :, :, lanes_of(path)] = total
            else:
                part[k, :, here, :, lanes_of(path)] = total
            for i in range(3):
                to = near(there, TO[i])
                row = (here, to) if path == 0 else (to, here)
                send3[path, k, i] = part[k, row[0], row[1], :, lanes_of(path)].astype(BF)
                send(send3.at[path, k, i], recv3.at[path, k, i], s3.at[path, k, i], r3.at[path, k, i], along(axes[path][1], TO[i]))

    def stage3(k):
        for path in (0, 1):
            for i in range(3):
                got(recv3.at[path, k, i], s3.at[path, k, i], r3.at[path, k, i], along(axes[path][1], TO[i]))
            total = part[k, z, x, :, lanes_of(path)]
            for i in range(3):
                total = total + recv3[path, k, i].astype(F32)
            columns = columns_of(path, k)
            grad_v[:, columns] = total
            norm[z, x, :, columns] = step_of(*adam(total, first_v[:, columns], second_v[:, columns]))
            own = norm.at[z, x, :, columns]
            for i in range(3):
                send(own, own, s5.at[path, k, i], r5.at[path, k, i], along(axes[path][1], TO[i]))

    def stage4(k):
        for path in (0, 1):
            columns = columns_of(path, k)
            for i in range(3):
                got(norm.at[0, 0, :, columns], s5.at[path, k, i], r5.at[path, k, i], along(axes[path][1], TO[i]))
            block = slab(norm, path, places[path][0]).at[:, :, columns]
            for d in (0, 1):
                send(block, block, s7.at[path, k, d], r7.at[path, k, d], along(axes[path][0], TO[d]))

    def stage5(k):
        for path in (0, 1):
            columns = columns_of(path, k)
            for d in (0, 1):
                place = near(places[path][0], FROM[1 + d])
                got(slab(norm, path, place).at[:, :, columns], s7.at[path, k, d], r7.at[path, k, d], along(axes[path][0], TO[d]))
                block = slab(norm, path, place, 2 * d, 2).at[:, :, columns]
                send(block, block, s8.at[path, k, d], r8.at[path, k, d], along(axes[path][0], TO[d]))

    def stage6(k):
        for path in (0, 1):
            columns = columns_of(path, k)
            for d in (0, 1):
                place = near(places[path][0], 2)
                got(slab(norm, path, place, 2 * d, 2).at[:, :, columns], s8.at[path, k, d], r8.at[path, k, d], along(axes[path][0], TO[d]))
        columns = pl.ds(k * width, width)
        store(norm.at[:, :, :, columns], norm_out.at[:, :, :, columns], k)

    stages = (stage0, stage1, stage2, stage3, stage4, stage5, stage6)
    summed = 0
    for stage, k in ORDER:
        stages[stage](k)
        if stage == 3:
            summed += 1
            if summed == CHUNKS:
                store(grad_v, grad_out, CHUNKS + 1)
    for copy in sent:
        copy.wait_send()
    for copy in stores:
        copy.wait()


def finish(norm, rows, grad, first, second, grad_out, first_out, second_out, update):
    grad_out[...] = grad[...]
    first_out[...], second_out[...] = adam(grad[...], first[...], second[...])
    update[...] = jnp.dot(rows[...], norm[...], preferred_element_type=F32).astype(BF)


def local(acts, grads, basis, first, second):
    tokens, width = acts.shape
    rows, rank = basis.shape
    own, units = first.shape
    wide = units // CHUNKS
    half = wide // 2
    pairs = (2, CHUNKS)
    vmem, dma = pltpu.VMEM, pltpu.SemaphoreType.DMA
    whole = pl.BlockSpec(memory_space=pl.ANY)
    norm, rows_all, grad = pl.pallas_call(
        exchange,
        out_shape=(
            jax.ShapeDtypeStruct((SIDE, SIDE, own, units), BF),
            jax.ShapeDtypeStruct((rows, 8 * rank), BF),
            jax.ShapeDtypeStruct((own, units), F32),
        ),
        in_specs=[whole] * 5,
        out_specs=[whole] * 3,
        scratch_shapes=[
            vmem((16, tokens, rows), BF),
            vmem((CHUNKS, tokens, wide), BF),
            vmem((rows, rank), BF),
            vmem((own, units), F32),
            vmem((own, units), F32),
            vmem((SIDE, SIDE, rows // 2, 2 * rank), BF),
            vmem((8, rows // 2, 2 * rank), BF),
            vmem((rows, 8 * rank), BF),
            vmem((2, tokens, 2 * rank), F32),
            vmem((8, rank, tokens), BF),
            vmem((CHUNKS, SIDE, SIDE, own, wide), F32),
            vmem((*pairs, 2, 2, own, half), BF),
            vmem((*pairs, 2, SIDE, own, half), BF),
            vmem((*pairs, 3, own, half), BF),
            vmem((*pairs, 2, 2, own, half), BF),
            vmem((*pairs, 2, SIDE, own, half), BF),
            vmem((*pairs, 3, own, half), BF),
            vmem((SIDE, SIDE, own, units), BF),
            vmem((own, units), F32),
            dma((19 + CHUNKS,)),
            dma((2, 3)), dma((2, 3)), dma((2, 4, 3)), dma((2, 4, 3)),
            dma((7,)), dma((7,)), dma((7,)), dma((7,)),
            dma((*pairs, 2)), dma((*pairs, 2)), dma((*pairs, 2)), dma((*pairs, 2)),
            dma((*pairs, 3)), dma((*pairs, 3)), dma((*pairs, 3)), dma((*pairs, 3)),
            dma((*pairs, 2)), dma((*pairs, 2)), dma((*pairs, 2)), dma((*pairs, 2)),
            dma((CHUNKS + 2,)),
        ],
        compiler_params=pltpu.CompilerParams(
            collective_id=0, has_side_effects=True, vmem_limit_bytes=60 << 20
        ),
        name="exchange",
    )(acts, grads, basis, first, second)
    columns = lambda n: pl.BlockSpec((n, wide), lambda k: (0, k))
    return pl.pallas_call(
        finish,
        grid=(CHUNKS,),
        out_shape=(
            jax.ShapeDtypeStruct((own, units), F32),
            jax.ShapeDtypeStruct((own, units), F32),
            jax.ShapeDtypeStruct((own, units), F32),
            jax.ShapeDtypeStruct((rows, units), BF),
        ),
        in_specs=[
            columns(16 * own),
            pl.BlockSpec((rows, 8 * rank), lambda k: (0, 0)),
            columns(own),
            columns(own),
            columns(own),
        ],
        out_specs=(columns(own), columns(own), columns(own), columns(rows)),
        compiler_params=pltpu.CompilerParams(vmem_limit_bytes=32 << 20),
        name="finish",
    )(norm.reshape(16 * own, units), rows_all, grad, first, second)


def solution(mesh):
    both = P("dp", "tensor")
    return jax.shard_map(
        local,
        mesh=mesh,
        in_specs=(P("dp", None), both, both, both, both),
        out_specs=(both, both, both, both),
        check_vma=False,
    )
```

time: 287 us -> 86.8 us (0.30)
  waiting for transfers between devices: 212 us -> 0 us
  Pallas kernels: 0 us -> 79 us
  matrix products: 37.3 us -> 0 us
  blocking collectives: 15 us -> 0 us
  between operations: 13.8 us -> 0.67 us
    all_gather x2 -> x0, waiting for transfers between devices: 130 us -> none  [the longest x1 80.3 us: local(): lax.all_gather(rows_block, 'dp', axis=0, tiled=True)]
    reduce_scatter x1 -> x0, waiting for transfers between devices: 82.3 us -> none  [local(): lax.psum_scatter(jnp.einsum('tr,tf->rf', projected, output_grads, preferr...]
    pallas_call x0 -> x2, Pallas kernels: none -> 79 us  [the longest x1 73.8 us: local(): pl.pallas_call(exchange, out_shape=(jax.ShapeDtypeStruct((SIDE, SIDE, own...]
    dot_general x2 -> x0, matrix products: 37.3 us -> none  [the longest x1 31.3 us: local(): jnp.einsum('tr,tf->rf', projected, output_grads, preferred_element_type=j...]
    all_gather x1 -> x0, blocking collectives: 15 us -> none  [local(): rows_block = lax.all_gather(basis, 'tensor', axis=1, tiled=True)]
    unnamed x7 -> x11, local copies, waits for them, and re-layouts: 5.92 us -> 5.7 us
  transfers between devices with their start and end apart: 3 -> 0, of which waited for: 3 -> 0; matrix products, arithmetic and copies ran while one was open for 0% -> 0% of each run, Pallas kernels for 0% -> 0%
where the time goes in v1:
time: 86.8 us; the launch traced here: 85.3 us
  Pallas kernels  79 us (91%)
  local copies, waits for them, and re-layouts  5.7 us (7%)
    pallas_call x1, Pallas kernels, local(): pl.pallas_call(exchange, out_shape=(jax.ShapeDtypeStruct((SIDE, SIDE, own...  73.8 us
    unnamed x11, local copies, waits for them, and re-layouts  5.7 us
    pallas_call x1, Pallas kernels, local(): pl.pallas_call(finish, grid=(CHUNKS,), out_shape=(jax.ShapeDtypeStruct((o...  5.16 us

profile of v1, /device:TPU:0, one launch (start us, length us, event | category | flops | bytes accessed | tf_op | source)
XLA Modules:
  0.0 85.3 jit_solution(6520830803957504956)
XLA Ops:
  0.6 1.6 %copy.9.basis = bf16[512,64]{1,0:T(8,128)(2,1)} copy(bf16[512,64]{0,1:T(8,128)(2,1)} %param.7) | data formatting | bytes 131072 | tf_op args[2]
  2.2 0.0 copy-start.1
  2.2 0.0 copy-start.2
  2.2 73.8 %exchange.1 = (bf16[4,4,32,3584]{3,2,1,0:T(8,128)(2,1)}, bf16[512,512]{1,0:T(8,128)(2,1)}, f32[32,3584]{1,0:T(8,128)}) custom-call(bf16[1024,8192]{1,0:T(8,128)(2,1)} %acts.1, bf16[1024,3584]{1,0:T(8,128)(2,1)} %grads.1, bf16[512,64]{1,0:T(8,128)(2,1)} %copy.9.basis, f32[32,3584]{1,0:T(8,128)} %first.3, f32[32,3584]{1,0:T(8,128)} %second.3), custom_call_target="tpu_custom_call" | custom-call | tf_op jit(solution)/shard_map/exchange/pallas_call | solution.py:335
  76.1 0.0 copy-done.1
  76.1 0.0 copy-done.2
  76.1 0.0 copy-start
  76.1 2.0 %copy-done = bf16[4,4,32,3584]{3,2,1,0:T(8,128)(2,1)S(1)} copy-done((bf16[4,4,32,3584]{3,2,1,0:T(8,128)(2,1)S(1)}, bf16[4,4,32,3584]{3,2,1,0:T(8,128)(2,1)}, u32[]{:S(2)}) %copy-start) | copy-done | bytes 3670040
  78.1 0.0 copy-start.3
  78.1 1.0 %copy-done.3 = bf16[512,512]{1,0:T(8,128)(2,1)S(1)} copy-done((bf16[512,512]{1,0:T(8,128)(2,1)S(1)}, bf16[512,512]{1,0:T(8,128)(2,1)}, u32[]{:S(2)}) %copy-start.3) | copy-done | bytes 524312
  79.2 0.0 copy-start.4
  79.2 1.0 %copy-done.4 = f32[32,3584]{1,0:T(8,128)S(1)} copy-done((f32[32,3584]{1,0:T(8,128)S(1)}, f32[32,3584]{1,0:T(8,128)}, u32[]{:S(2)}) %copy-start.4) | copy-done | bytes 458776
  80.2 5.2 %finish.1 = (f32[32,3584]{1,0:T(8,128)}, f32[32,3584]{1,0:T(8,128)}, f32[32,3584]{1,0:T(8,128)}, bf16[512,3584]{1,0:T(8,128)(2,1)}) custom-call(bf16[512,3584]{1,0:T(8,128)(2,1)S(1)} %bitcast.1, bf16[512,512]{1,0:T(8,128)(2,1)S(1)} %copy-done.3, f32[32,3584]{1,0:T(8,128)S(1)} %copy-done.4, f32[32,3584]{1,0:T(8,128)S(1)} %copy-done.1, f32[32,3584]{1,0:T(8,128)S(1)} %copy-done.2), custom_call_target="tpu_custom_call" | custom-call | tf_op jit(solution)/shard_map/finish/pallas_call | solution.py:378
Async XLA Ops:
  2.2 73.8 %copy-start.1 = (f32[32,3584]{1,0:T(8,128)S(1)}, f32[32,3584]{1,0:T(8,128)}, u32[]{:S(2)}) copy-start(f32[32,3584]{1,0:T(8,128)} %first.3) | copy-start | bytes 1376260
  2.2 73.8 %copy-start.2 = (f32[32,3584]{1,0:T(8,128)S(1)}, f32[32,3584]{1,0:T(8,128)}, u32[]{:S(2)}) copy-start(f32[32,3584]{1,0:T(8,128)} %second.3) | copy-start | bytes 1376260
  76.1 2.0 %copy-start = (bf16[4,4,32,3584]{3,2,1,0:T(8,128)(2,1)S(1)}, bf16[4,4,32,3584]{3,2,1,0:T(8,128)(2,1)}, u32[]{:S(2)}) copy-start(bf16[4,4,32,3584]{3,2,1,0:T(8,128)(2,1)} %get-tuple-element.7) | copy-start | bytes 11010052
  78.1 1.0 %copy-start.3 = (bf16[512,512]{1,0:T(8,128)(2,1)S(1)}, bf16[512,512]{1,0:T(8,128)(2,1)}, u32[]{:S(2)}) copy-start(bf16[512,512]{1,0:T(8,128)(2,1)} %get-tuple-element.8.rows) | copy-start | bytes 1572868
  79.2 1.0 %copy-start.4 = (f32[32,3584]{1,0:T(8,128)S(1)}, f32[32,3584]{1,0:T(8,128)}, u32[]{:S(2)}) copy-start(f32[32,3584]{1,0:T(8,128)} %get-tuple-element.9.grad) | copy-start | bytes 1376260

commit v2 on v0

v2 whole, which is shorter than its diff:
```python
import functools

import jax
import jax.numpy as jnp
from jax import lax
from jax.experimental import pallas as pl
from jax.experimental.pallas import tpu as pltpu
from jax.sharding import PartitionSpec as P

STEP = 1000

beta_one = 0.9
beta_two = 0.999
adam_eps = 1e-08

MESH = pl.DeviceIdType.MESH
BF = jnp.bfloat16
F32 = jnp.float32

SIDE = 4
TO = (1, -1, 2)
FROM = (0, -1, 1, 2)

PIECE = 512
UNITS = [
    (0, 0, 512), (0, 512, 1024), (0, 1536, 1024), (0, 2560, 1024),
    (1, 0, 1024), (1, 1024, 1024), (1, 2048, 1024), (1, 3072, 512),
]
ORDER = [
    (0, 0), (0, 1), (7, 0), (0, 2), (1, 0), (0, 3), (1, 1), (8, 0),
    (0, 4), (1, 2), (2, 0), (0, 5), (1, 3), (2, 1), (0, 6), (1, 4), (2, 2), (0, 7), (3, 0),
    (1, 5), (2, 3), (3, 1), (1, 6), (2, 4), (3, 2), (1, 7), (2, 5), (3, 3), (4, 0),
    (2, 6), (3, 4), (4, 1), (2, 7), (3, 5), (4, 2), (3, 6), (5, 0), (4, 3), (3, 7), (5, 1),
    (4, 4), (5, 2), (4, 5), (5, 3), (4, 6), (5, 4), (4, 7), (5, 5), (6, 0), (6, 1), (6, 2),
    (5, 6), (5, 7), (6, 3), (6, 4), (6, 5), (6, 6), (6, 7),
]


def adam(grad, first, second):
    first_out = beta_one * first + (1.0 - beta_one) * grad
    second_out = beta_two * second + (1.0 - beta_two) * grad * grad
    return first_out, second_out


def step_of(first_out, second_out):
    first_hat = first_out / (1.0 - beta_one**STEP)
    second_hat = second_out / (1.0 - beta_two**STEP)
    return (first_hat / (jnp.sqrt(second_hat) + adam_eps)).astype(BF)


def exchange(
    acts, grads, basis, first, second,
    norm, rows_v, grad_v, first_o, second_o,
    act_v, grads_v, basis_v, first_v, second_v, packs, rows_packs, acc, turned,
    part, send1, send2, send3, recv1, recv2, recv3,
    load_s, send_s, hop_r, block_r, tensor_r, unit_r,
):
    dp, tensor = lax.axis_index("dp"), lax.axis_index("tensor")
    z, x, y, core = dp // SIDE, dp % SIDE, tensor // 2, tensor % 2
    depth = act_v.shape[2]
    own = norm.shape[2] // 2

    def near(at, step):
        return lax.rem(at + step + SIDE, SIDE)

    def along(axis, step):
        if axis == "z":
            return (near(z, step) * SIDE + x, tensor)
        if axis == "x":
            return (z * SIDE + near(x, step), tensor)
        if axis == "y":
            return (dp, near(y, step) * 2 + core)
        return (dp, y * 2 + (1 - core))

    def send(ref, to, kind, rsem, device):
        pltpu.make_async_remote_copy(
            src_ref=ref, dst_ref=to, send_sem=send_s.at[kind], recv_sem=rsem,
            device_id=device, device_id_type=MESH,
        ).start()

    def got(like, rsem):
        pltpu.make_async_remote_copy(
            src_ref=like, dst_ref=like, send_sem=send_s.at[0], recv_sem=rsem,
            device_id=along("core", 1), device_id_type=MESH,
        ).wait_recv()

    def all_sent(like, kind):
        pltpu.make_async_remote_copy(
            src_ref=like, dst_ref=like, send_sem=send_s.at[kind], recv_sem=unit_r.at[0, 0],
            device_id=along("core", 1), device_id_type=MESH,
        ).wait_send()

    def load(src, dst, n):
        copy = pltpu.make_async_copy(src, dst, load_s.at[n])
        copy.start()
        return copy

    order = [(0, 0), (0, 1), (0, 2), (1, 0), (2, 0), (0, 3), (3, 0)]
    order += [(a, b) for a in (1, 2) for b in (1, 2)]
    order += [(1, 3), (2, 3), (3, 1), (3, 2), (3, 3)]
    loaded_basis = load(basis, basis_v, 0)
    for n, (a, b) in enumerate(order):
        block = near(z, FROM[a]) * SIDE + near(x, FROM[b])
        columns = pl.ds(pl.multiple_of(block * depth, depth), depth)
        load(acts.at[:, columns], act_v.at[n], 1 + n // 2)

    barrier = pltpu.get_barrier_semaphore()
    partners = [along(axis, step) for axis in "zxy" for step in TO] + [along("core", 1)]
    for device in partners:
        pl.semaphore_signal(barrier, inc=1, device_id=device, device_id_type=MESH)
    loaded_basis.wait()
    rows_packs[tensor] = basis_v[...]
    for h in (0, 1):
        packs[h, z, x, :own] = basis_v[h * own : (h + 1) * own]
        packs[h, z, x, own:] = basis_v[(h + 2) * own : (h + 3) * own]
    pl.semaphore_wait(barrier, len(partners))

    lead, trail = ("x", "z"), ("z", "x")

    def spot(h, path, m, i):
        a, b = (i, m) if path == 0 else (m, i)
        return packs.at[h, near(z, FROM[a]), near(x, FROM[b]), pl.ds(path * own, own)]

    def onward(h, path, m):
        block = spot(h, path, m, 0)
        for i in range(3):
            n = order.index((i + 1, m) if path == 0 else (m, i + 1))
            send(block, block, 0, block_r.at[h, n], along(trail[path], TO[i]))

    def outset(h):
        for path in (0, 1):
            block = spot(h, path, 0, 0)
            for i in range(3):
                send(block, block, 0, hop_r.at[h, i], along(lead[path], TO[i]))
        for path in (0, 1):
            onward(h, path, 0)

    def first_hop(h, m):
        got(packs.at[h, 0, 0], hop_r.at[h, m - 1])
        for path in (0, 1):
            onward(h, path, m)

    def project(h, n):
        a, b = order[n]
        if n > 0:
            halves = 2 if a > 0 and b > 0 else 1
            got(packs.at[h, 0, 0, pl.ds(0, halves * own)], block_r.at[h, n])
        if h == 0 and n % 2 == 0:
            two = act_v.at[pl.ds(n, 2)]
            pltpu.make_async_copy(two, two, load_s.at[1 + n // 2]).wait()
        block = packs[h, near(z, FROM[a]), near(x, FROM[b])]
        term = lax.dot_general(
            block, act_v[n], (((1,), (1,)), ((), ())), preferred_element_type=F32
        )
        acc[h] = term if n == 0 else acc[h] + term

    def spread(buffer, rsem):
        block = buffer.at[tensor]
        send(block, block, 1, rsem.at[3], along("core", 1))
        for i in range(3):
            send(block, block, 1, rsem.at[i], along("y", TO[i]))

    def forward(buffer, rsem):
        for i in range(3):
            block = buffer.at[near(y, FROM[1 + i]) * 2 + core]
            got(block, rsem.at[i])
            send(block, block, 1, rsem.at[3], along("core", 1))

    def collected(buffer, rsem):
        got(buffer.at[pl.ds(0, SIDE)], rsem.at[3])

    def rounded(h):
        turned[h, tensor] = acc[h].astype(BF)
        spread(turned.at[h], tensor_r.at[h])

    outset(0)
    spread(rows_packs, tensor_r.at[2])
    project(0, 0)
    for m in (1, 2, 3):
        first_hop(0, m)
    outset(1)
    for n in range(1, 7):
        project(0, n)
    for m in (1, 2, 3):
        first_hop(1, m)
    for n in range(7, 16):
        project(0, n)
    rounded(0)
    loaded_grads = []
    for u in range(len(UNITS) // 2):
        columns = pl.ds(*UNITS[u][1:])
        loaded_grads.append(load(grads.at[:, columns], grads_v.at[:, columns], 9 + u))
    loaded_moments = [load(first, first_v, 13), load(second, second_v, 14)]
    for n in range(0, 10):
        project(1, n)
    forward(turned.at[0], tensor_r.at[0])
    for n in range(10, 16):
        project(1, n)
    rounded(1)
    forward(rows_packs, tensor_r.at[2])
    collected(turned.at[0], tensor_r.at[0])

    axes = (("z", "x"), ("x", "z"))
    places = ((z, x), (x, z))

    def lanes(path, u, base):
        _, low, count = UNITS[u]
        return pl.ds(low + path * count // 2 if base else low // 2, count // 2)

    def slab(ref, path, place, low=0, count=SIDE):
        if path == 0:
            return ref.at[place, pl.ds(low, count)]
        return ref.at[pl.ds(low, count), place]

    def rows(u):
        return pl.ds(UNITS[u][0] * own, own)

    def partial(path, u, place, low=0, count=SIDE):
        ref = slab(part.at[UNITS[u][0]], path, place, low, count)
        return ref[:, :, lanes(path, u, True)]

    def message(buffer, path, u, n):
        return buffer.at[path, UNITS[u][0], n].at[..., lanes(path, u, False)]

    def take(like, u, kind):
        got(like.at[:, UNITS[u][0]].at[..., lanes(0, u, False)], unit_r.at[kind, u])

    def stage0(u):
        h, low, count = UNITS[u]
        if h == 0:
            loaded_grads[u].wait()
        lhs = turned[h].reshape(16 * own, turned.shape[3])
        product = jnp.dot(lhs, grads_v[:, low : low + count], preferred_element_type=F32)
        part[h, :, :, :, low : low + count] = product.reshape(SIDE, SIDE, own, count)
        for path in (0, 1):
            far = near(places[path][0], 2)
            for d in (0, 1):
                out = message(send1, path, u, d)
                out[...] = partial(path, u, far, 2 * d, 2).astype(BF)
                to = along(axes[path][0], TO[d])
                send(out, message(recv1, path, u, d), 2, unit_r.at[0, u], to)

    def stage1(u):
        take(recv1, u, 0)
        for path in (0, 1):
            for d in (0, 1):
                arrived = message(recv1, path, u, d)
                to = near(places[path][0], TO[d])
                out = message(send2, path, u, d)
                joined = partial(path, u, to, 2 * d, 2) + arrived[...].astype(F32)
                out[2 * d : 2 * d + 2] = joined.astype(BF)
                other = 2 - 2 * d
                out[other : other + 2] = partial(path, u, to, other, 2).astype(BF)
                to = along(axes[path][0], TO[d])
                send(out, message(recv2, path, u, d), 3, unit_r.at[1, u], to)

    def stage2(u):
        take(recv2, u, 1)
        for path in (0, 1):
            here, there = places[path]
            total = partial(path, u, here)
            for d in (0, 1):
                total = total + message(recv2, path, u, d)[...].astype(F32)
            ref = slab(part.at[UNITS[u][0]], path, here)
            columns = lanes(path, u, True)
            ref[:, :, columns] = total
            for i in range(3):
                out = message(send3, path, u, i)
                out[...] = ref[near(there, TO[i]), :, columns].astype(BF)
                to = along(axes[path][1], TO[i])
                send(out, message(recv3, path, u, i), 4, unit_r.at[2, u], to)

    def stage3(u):
        if u == 0:
            for copy in loaded_moments:
                copy.wait()
        take(recv3, u, 2)
        for path in (0, 1):
            columns = lanes(path, u, True)
            total = part[UNITS[u][0], z, x, :, columns]
            for i in range(3):
                total = total + message(recv3, path, u, i)[...].astype(F32)
            at = rows(u), columns
            moments = adam(total, first_v[at], second_v[at])
            grad_v[at] = total
            first_o[at], second_o[at] = moments
            norm[z, x, rows(u), columns] = step_of(*moments)
            block = norm.at[z, x, rows(u), columns]
            for i in range(3):
                send(block, block, 5, unit_r.at[3, u], along(axes[path][1], TO[i]))

    def stage4(u):
        take(recv3, u, 3)
        for path in (0, 1):
            block = slab(norm, path, places[path][0]).at[:, rows(u), lanes(path, u, True)]
            for d in (0, 1):
                send(block, block, 6, unit_r.at[4, u], along(axes[path][0], TO[d]))

    def stage5(u):
        take(recv2, u, 4)
        for path in (0, 1):
            for d in (0, 1):
                place = near(places[path][0], FROM[1 + d])
                block = slab(norm, path, place, 2 * d, 2).at[:, rows(u), lanes(path, u, True)]
                send(block, block, 7, unit_r.at[5, u], along(axes[path][0], TO[d]))

    def stage6(u):
        take(recv1, u, 5)

    def stage7(_):
        forward(turned.at[1], tensor_r.at[1])

    def stage8(_):
        collected(turned.at[1], tensor_r.at[1])
        collected(rows_packs, tensor_r.at[2])
        whole = rows_packs[...].reshape(rows_v.shape[1], rows_v.shape[0])
        rows_v[...] = whole.astype(F32).T.astype(BF)

    stages = (stage0, stage1, stage2, stage3, stage4, stage5, stage6, stage7, stage8)
    for stage, u in ORDER:
        stages[stage](u)
    all_sent(act_v.at[0, pl.ds(0, 2 * 30 * own)], 0)
    all_sent(act_v.at[pl.ds(0, 3), pl.ds(0, 7 * rows_packs.shape[1])], 1)
    for kind, like in ((2, send1), (3, send2), (4, send3), (5, send3), (6, send2), (7, send1)):
        all_sent(like, kind)


def finish(norm, rows, grad, first, second, grad_out, first_out, second_out, update, tiles, sems):
    copies = []

    def store(src, dst):
        copies.append(pltpu.make_async_copy(src, dst, sems.at[len(copies)]))
        copies[-1].start()

    wide = tiles.shape[2]
    for k in range(tiles.shape[0]):
        columns = pl.ds(k * wide, wide)
        tiles[k] = jnp.dot(rows[...], norm[:, columns], preferred_element_type=F32).astype(BF)
        store(tiles.at[k], update.at[:, columns])
        if k == 0:
            for src, dst in ((grad, grad_out), (first, first_out), (second, second_out)):
                store(src, dst)
    for copy in copies:
        copy.wait()


def local(acts, grads, basis, first, second):
    tokens = acts.shape[0]
    rank, rows = basis.shape
    own, units = first.shape
    pieces = units // PIECE
    vmem, dma = pltpu.VMEM, pltpu.SemaphoreType.DMA
    whole = pl.BlockSpec(memory_space=pl.ANY)
    norm, *rest = pl.pallas_call(
        exchange,
        out_shape=(
            vmem((SIDE, SIDE, own, units), BF),
            vmem((rows, 8 * rank), BF),
            vmem((own, units), F32),
            vmem((own, units), F32),
            vmem((own, units), F32),
        ),
        in_specs=[whole] * 5,
        out_specs=[pl.BlockSpec(memory_space=vmem)] * 5,
        scratch_shapes=[
            vmem((16, tokens, rows), BF),
            vmem((tokens, units), BF),
            vmem((rank, rows), BF),
            vmem((own, units), F32),
            vmem((own, units), F32),
            vmem((2, SIDE, SIDE, own, rows), BF),
            vmem((8, rank, rows), BF),
            vmem((2, own, tokens), F32),
            vmem((2, 8, own, tokens), BF),
            vmem((2, SIDE, SIDE, own // 2, units), F32),
            vmem((2, 2, 2, 2, own // 2, units // 2), BF),
            vmem((2, 2, 2, SIDE, own // 2, units // 2), BF),
            vmem((2, 2, 3, own // 2, units // 2), BF),
            vmem((2, 2, 2, 2, own // 2, units // 2), BF),
            vmem((2, 2, 2, SIDE, own // 2, units // 2), BF),
            vmem((2, 2, 3, own // 2, units // 2), BF),
            dma((15,)), dma((8,)), dma((2, 3)), dma((2, 16)), dma((3, 4)), dma((6, len(UNITS))),
        ],
        compiler_params=pltpu.CompilerParams(
            collective_id=0, has_side_effects=True, vmem_limit_bytes=50 << 20
        ),
        name="exchange",
    )(acts, grads, basis, first, second)
    return pl.pallas_call(
        finish,
        out_shape=(
            jax.ShapeDtypeStruct((own, units), F32),
            jax.ShapeDtypeStruct((own, units), F32),
            jax.ShapeDtypeStruct((own, units), F32),
            jax.ShapeDtypeStruct((rows, units), BF),
        ),
        in_specs=[pl.BlockSpec(memory_space=vmem)] * 5,
        out_specs=[pl.BlockSpec(memory_space=pltpu.HBM)] * 4,
        scratch_shapes=[vmem((pieces, rows, PIECE), BF), dma((pieces + 3,))],
        compiler_params=pltpu.CompilerParams(vmem_limit_bytes=16 << 20),
        name="finish",
    )(norm.reshape(16 * own, units), *rest)


def solution(mesh):
    both = P("dp", "tensor")

    def step(acts, grads, basis, first, second):
        return local(acts, grads, basis.T, first, second)

    return jax.shard_map(
        step,
        mesh=mesh,
        in_specs=(P("dp", None), both, both, both, both),
        out_specs=(both, both, both, both),
        check_vma=False,
    )
```

time: 287 us -> 77.9 us (0.27)
  waiting for transfers between devices: 212 us -> 0 us
  Pallas kernels: 0 us -> 77.2 us
  matrix products: 37.3 us -> 0 us
  blocking collectives: 15 us -> 0 us
  between operations: 13.8 us -> 0.64 us
  local copies, waits for them, and re-layouts: 5.92 us -> 0 us
    all_gather x2 -> x0, waiting for transfers between devices: 130 us -> none  [the longest x1 80.3 us: local(): lax.all_gather(rows_block, 'dp', axis=0, tiled=True)]
    reduce_scatter x1 -> x0, waiting for transfers between devices: 82.3 us -> none  [local(): lax.psum_scatter(jnp.einsum('tr,tf->rf', projected, output_grads, preferr...]
    pallas_call x0 -> x2, Pallas kernels: none -> 77.2 us  [the longest x1 74.2 us: local(): pl.pallas_call(exchange, out_shape=(vmem((SIDE, SIDE, own, units), BF), v...]
    dot_general x2 -> x0, matrix products: 37.3 us -> none  [the longest x1 31.3 us: local(): jnp.einsum('tr,tf->rf', projected, output_grads, preferred_element_type=j...]
    all_gather x1 -> x0, blocking collectives: 15 us -> none  [local(): rows_block = lax.all_gather(basis, 'tensor', axis=1, tiled=True)]
    unnamed x7 -> x0, local copies, waits for them, and re-layouts: 5.92 us -> none
  transfers between devices with their start and end apart: 3 -> 0, of which waited for: 3 -> 0; matrix products, arithmetic and copies ran while one was open for 0% -> 0% of each run, Pallas kernels for 0% -> 0%
where the time goes in v2:
time: 77.9 us; the launch traced here: 77.8 us
  Pallas kernels  77.2 us (99%)
    pallas_call x1, Pallas kernels, local(): pl.pallas_call(exchange, out_shape=(vmem((SIDE, SIDE, own, units), BF), v...  74.2 us
    pallas_call x1, Pallas kernels, local(): pl.pallas_call(finish, out_shape=(jax.ShapeDtypeStruct((own, units), F32)...  2.96 us

profile of v2, /device:TPU:0, one launch (start us, length us, event | category | flops | bytes accessed | tf_op | source)
XLA Modules:
  0.0 77.8 jit_solution(14960215666698500936)
XLA Ops:
  0.6 74.2 %exchange.1 = (bf16[4,4,32,3584]{3,2,1,0:T(8,128)(2,1)S(1)}, bf16[512,512]{1,0:T(8,128)(2,1)S(1)}, f32[32,3584]{1,0:T(8,128)S(1)}, f32[32,3584]{1,0:T(8,128)S(1)}, f32[32,3584]{1,0:T(8,128)S(1)}) custom-call(bf16[1024,8192]{1,0:T(8,128)(2,1)} %acts.1, bf16[1024,3584]{1,0:T(8,128)(2,1)} %grads.1, bf16[64,512]{1,0:T(8,128)(2,1)} %bitcast.3, f32[32,3584]{1,0:T(8,128)} %first.1, ...), custom_call_target="tpu_custom_call" | custom-call | tf_op jit(solution)/shard_map/exchange/pallas_call | solution.py:354
  74.8 3.0 %finish.1 = (f32[32,3584]{1,0:T(8,128)}, f32[32,3584]{1,0:T(8,128)}, f32[32,3584]{1,0:T(8,128)}, bf16[512,3584]{1,0:T(8,128)(2,1)}) custom-call(bf16[512,3584]{1,0:T(8,128)(2,1)S(1)} %bitcast.2, bf16[512,512]{1,0:T(8,128)(2,1)S(1)} %get-tuple-element.10.rows, f32[32,3584]{1,0:T(8,128)S(1)} %get-tuple-element.11.grad, ...), custom_call_target="tpu_custom_call" | custom-call | tf_op jit(solution)/shard_map/finish/pallas_call | solution.py:389

commit v3 on v2

--- a/solution.py
+++ b/solution.py
@@ -27,12 +27,12 @@
     (1, 0, 1024), (1, 1024, 1024), (1, 2048, 1024), (1, 3072, 512),
 ]
 ORDER = [
-    (0, 0), (0, 1), (7, 0), (0, 2), (1, 0), (0, 3), (1, 1), (8, 0),
-    (0, 4), (1, 2), (2, 0), (0, 5), (1, 3), (2, 1), (0, 6), (1, 4), (2, 2), (0, 7), (3, 0),
-    (1, 5), (2, 3), (3, 1), (1, 6), (2, 4), (3, 2), (1, 7), (2, 5), (3, 3), (4, 0),
-    (2, 6), (3, 4), (4, 1), (2, 7), (3, 5), (4, 2), (3, 6), (5, 0), (4, 3), (3, 7), (5, 1),
-    (4, 4), (5, 2), (4, 5), (5, 3), (4, 6), (5, 4), (4, 7), (5, 5), (6, 0), (6, 1), (6, 2),
-    (5, 6), (5, 7), (6, 3), (6, 4), (6, 5), (6, 6), (6, 7),
+    (0, 0), (0, 1), (0, 2), (0, 3), (7, 0), (1, 0), (1, 1), (1, 2), (8, 0), (0, 4),
+    (0, 5), (0, 6), (0, 7), (1, 3), (2, 0), (2, 1), (1, 4), (1, 5), (1, 6), (1, 7),
+    (2, 2), (2, 3), (3, 0), (2, 4), (3, 1), (2, 5), (2, 6), (2, 7), (3, 2), (3, 3),
+    (3, 4), (4, 0), (3, 5), (3, 6), (3, 7), (4, 1), (4, 2), (4, 3), (4, 4), (5, 0),
+    (4, 5), (4, 6), (4, 7), (5, 1), (5, 2), (5, 3), (5, 4), (6, 0), (5, 5), (5, 6),
+    (5, 7), (6, 1), (6, 2), (6, 3), (6, 4), (6, 5), (6, 6), (6, 7),
 ]
 
 
@@ -156,9 +156,9 @@
 
     def spread(buffer, rsem):
         block = buffer.at[tensor]
+        for i in (2, 0, 1):
+            send(block, block, 1, rsem.at[i], along("y", TO[i]))
         send(block, block, 1, rsem.at[3], along("core", 1))
-        for i in range(3):
-            send(block, block, 1, rsem.at[i], along("y", TO[i]))
 
     def forward(buffer, rsem):
         for i in range(3):
@@ -179,18 +179,19 @@
     for m in (1, 2, 3):
         first_hop(0, m)
     outset(1)
-    for n in range(1, 7):
+    for n in range(1, 11):
         project(0, n)
-    for m in (1, 2, 3):
-        first_hop(1, m)
-    for n in range(7, 16):
+    first_hop(1, 1)
+    first_hop(1, 2)
+    for n in range(11, 16):
         project(0, n)
     rounded(0)
+    first_hop(1, 3)
     loaded_grads = []
-    for u in range(len(UNITS) // 2):
+    for u in range(sum(unit[0] == 0 for unit in UNITS)):
         columns = pl.ds(*UNITS[u][1:])
-        loaded_grads.append(load(grads.at[:, columns], grads_v.at[:, columns], 9 + u))
-    loaded_moments = [load(first, first_v, 13), load(second, second_v, 14)]
+        loaded_grads.append(load(grads.at[:, columns], grads_v.at[:, columns], 11 + u))
+    loaded_moments = [load(first, first_v, 9), load(second, second_v, 10)]
     for n in range(0, 10):
         project(1, n)
     forward(turned.at[0], tensor_r.at[0])
@@ -333,13 +334,12 @@
         copies[-1].start()
 
     wide = tiles.shape[2]
+    for src, dst in ((grad, grad_out), (first, first_out), (second, second_out)):
+        store(src, dst)
     for k in range(tiles.shape[0]):
         columns = pl.ds(k * wide, wide)
         tiles[k] = jnp.dot(rows[...], norm[:, columns], preferred_element_type=F32).astype(BF)
         store(tiles.at[k], update.at[:, columns])
-        if k == 0:
-            for src, dst in ((grad, grad_out), (first, first_out), (second, second_out)):
-                store(src, dst)
     for copy in copies:
         copy.wait()
 
@@ -379,7 +379,7 @@
             vmem((2, 2, 2, 2, own // 2, units // 2), BF),
             vmem((2, 2, 2, SIDE, own // 2, units // 2), BF),
             vmem((2, 2, 3, own // 2, units // 2), BF),
-            dma((15,)), dma((8,)), dma((2, 3)), dma((2, 16)), dma((3, 4)), dma((6, len(UNITS))),
+            dma((11 + len(UNITS),)), dma((8,)), dma((2, 3)), dma((2, 16)), dma((3, 4)), dma((6, len(UNITS))),
         ],
         compiler_params=pltpu.CompilerParams(
             collective_id=0, has_side_effects=True, vmem_limit_bytes=50 << 20

time: 77.9 us -> 71 us (0.911)
  Pallas kernels: 77.2 us -> 70.1 us
    pallas_call x1, Pallas kernels: 74.2 us -> 67.1 us  [local(): pl.pallas_call(exchange, out_shape=(vmem((SIDE, SIDE, own, units), BF), v...]
where the time goes in v3:
time: 71 us; the launch traced here: 70.7 us
  Pallas kernels  70.1 us (99%)
    pallas_call x1, Pallas kernels, local(): pl.pallas_call(exchange, out_shape=(vmem((SIDE, SIDE, own, units), BF), v...  67.1 us
    pallas_call x1, Pallas kernels, local(): pl.pallas_call(finish, out_shape=(jax.ShapeDtypeStruct((own, units), F32)...  2.96 us

profile of v3, /device:TPU:0, one launch (start us, length us, event | category | flops | bytes accessed | tf_op | source)
XLA Modules:
  0.0 70.7 jit_solution(7680202440253527536)
XLA Ops:
  0.6 67.1 %exchange.1 = (bf16[4,4,32,3584]{3,2,1,0:T(8,128)(2,1)S(1)}, bf16[512,512]{1,0:T(8,128)(2,1)S(1)}, f32[32,3584]{1,0:T(8,128)S(1)}, f32[32,3584]{1,0:T(8,128)S(1)}, f32[32,3584]{1,0:T(8,128)S(1)}) custom-call(bf16[1024,8192]{1,0:T(8,128)(2,1)} %acts.1, bf16[1024,3584]{1,0:T(8,128)(2,1)} %grads.1, bf16[64,512]{1,0:T(8,128)(2,1)} %bitcast.3, f32[32,3584]{1,0:T(8,128)} %first.1, ...), custom_call_target="tpu_custom_call" | custom-call | tf_op jit(solution)/shard_map/exchange/pallas_call | solution.py:354
  67.8 3.0 %finish.1 = (f32[32,3584]{1,0:T(8,128)}, f32[32,3584]{1,0:T(8,128)}, f32[32,3584]{1,0:T(8,128)}, bf16[512,3584]{1,0:T(8,128)(2,1)}) custom-call(bf16[512,3584]{1,0:T(8,128)(2,1)S(1)} %bitcast.2, bf16[512,512]{1,0:T(8,128)(2,1)S(1)} %get-tuple-element.10.rows, f32[32,3584]{1,0:T(8,128)S(1)} %get-tuple-element.11.grad, ...), custom_call_target="tpu_custom_call" | custom-call | tf_op jit(solution)/shard_map/finish/pallas_call | solution.py:389

commit v4 on v3

--- a/solution.py
+++ b/solution.py
@@ -99,15 +99,20 @@
     order += [(a, b) for a in (1, 2) for b in (1, 2)]
     order += [(1, 3), (2, 3), (3, 1), (3, 2), (3, 3)]
     loaded_basis = load(basis, basis_v, 0)
-    for n, (a, b) in enumerate(order):
-        block = near(z, FROM[a]) * SIDE + near(x, FROM[b])
-        columns = pl.ds(pl.multiple_of(block * depth, depth), depth)
-        load(acts.at[:, columns], act_v.at[n], 1 + n // 2)
 
     barrier = pltpu.get_barrier_semaphore()
     partners = [along(axis, step) for axis in "zxy" for step in TO] + [along("core", 1)]
     for device in partners:
         pl.semaphore_signal(barrier, inc=1, device_id=device, device_id_type=MESH)
+
+    def load_acts(low, high):
+        for n in range(low, high):
+            a, b = order[n]
+            block = near(z, FROM[a]) * SIDE + near(x, FROM[b])
+            columns = pl.ds(pl.multiple_of(block * depth, depth), depth)
+            load(acts.at[:, columns], act_v.at[n], 1 + n // 2)
+
+    load_acts(0, 6)
     loaded_basis.wait()
     rows_packs[tensor] = basis_v[...]
     for h in (0, 1):
@@ -174,6 +179,7 @@
         spread(turned.at[h], tensor_r.at[h])
 
     outset(0)
+    load_acts(6, 16)
     spread(rows_packs, tensor_r.at[2])
     project(0, 0)
     for m in (1, 2, 3):

time: 71 us -> 71 us (level)
  no operation moved by 1% of the time
where the time goes in v4:
time: 71 us; the launch traced here: 70.7 us
  Pallas kernels  70.1 us (99%)
    pallas_call x1, Pallas kernels, local(): pl.pallas_call(exchange, out_shape=(vmem((SIDE, SIDE, own, units), BF), v...  67.1 us
    pallas_call x1, Pallas kernels, local(): pl.pallas_call(finish, out_shape=(jax.ShapeDtypeStruct((own, units), F32)...  2.96 us

profile of v4, /device:TPU:0, one launch (start us, length us, event | category | flops | bytes accessed | tf_op | source)
XLA Modules:
  0.0 70.7 jit_solution(8570067454171234044)
XLA Ops:
  0.6 67.1 %exchange.1 = (bf16[4,4,32,3584]{3,2,1,0:T(8,128)(2,1)S(1)}, bf16[512,512]{1,0:T(8,128)(2,1)S(1)}, f32[32,3584]{1,0:T(8,128)S(1)}, f32[32,3584]{1,0:T(8,128)S(1)}, f32[32,3584]{1,0:T(8,128)S(1)}) custom-call(bf16[1024,8192]{1,0:T(8,128)(2,1)} %acts.1, bf16[1024,3584]{1,0:T(8,128)(2,1)} %grads.1, bf16[64,512]{1,0:T(8,128)(2,1)} %bitcast.3, f32[32,3584]{1,0:T(8,128)} %first.1, ...), custom_call_target="tpu_custom_call" | custom-call | tf_op jit(solution)/shard_map/exchange/pallas_call | solution.py:360
  67.7 3.0 %finish.1 = (f32[32,3584]{1,0:T(8,128)}, f32[32,3584]{1,0:T(8,128)}, f32[32,3584]{1,0:T(8,128)}, bf16[512,3584]{1,0:T(8,128)(2,1)}) custom-call(bf16[512,3584]{1,0:T(8,128)(2,1)S(1)} %bitcast.2, bf16[512,512]{1,0:T(8,128)(2,1)S(1)} %get-tuple-element.10.rows, f32[32,3584]{1,0:T(8,128)S(1)} %get-tuple-element.11.grad, ...), custom_call_target="tpu_custom_call" | custom-call | tf_op jit(solution)/shard_map/finish/pallas_call | solution.py:395
